TPU v7x, 32 devices: a whole 2x2x4 slice. The times are simulated.
32 devices in a mesh: groups: 2 (over y), dp: 4 (over z), mp: 2 (over x), layer: 2 (over core).
Axes of the slice: x: 2, y: 2, z: 4, core: 2. Of those that a mesh axis runs over, the one named last changes fastest.
Arguments:
- acts: bfloat16 [2, 4096, 8192], P('layer', ('groups', 'dp'), 'mp'), parts along dimension 1, may hold values from -6 to 6
- grads: bfloat16 [2, 4096, 28672], P('layer', ('groups', 'dp'), 'mp'), parts along dimension 1, may hold values from -6 to 6
- query_left: bfloat16 [2, 8192, 512], P('layer', ('mp', 'dp'), 'groups'), parts along dimension 2, may hold values from -0.0625 to 0.0625
- query_right: bfloat16 [2, 28672, 512], P('layer', ('mp', 'dp'), 'groups'), parts along dimension 2, may hold values from -0.03125 to 0.03125
- seq_len: int32 [16], P(('groups', 'dp')), parts along dimension 0, may hold values from 1 to 256, 1024 in all
Outputs:
- scores: float32 [2, 16, 32], P('layer', ('groups', 'dp')), parts along dimension 1
There are 2 independent parts, one for each index of `groups`. A program takes and returns all parts, laid end to end along the dimension named above; each array names one. Nothing has to cross between parts.
Inputs may be any that keep to these rules, and one draw needn't show every extreme that they name: `seq_len`: every sequence has at least one live token and some sequence has exactly 256.
All inputs are finite; a program needn't handle non-finite values. No bound on the sum of `seq_len` on one device may be relied on, other than what follows from the above.
Results may differ from a plain program's by a relative error of at most 0.0003.
Values may be sent and summed in bfloat16 or wider, within the bound.
No kernel may reach another device: no remote copies, remote signals or barrier semaphores. Data moves between devices by JAX's collectives and lax.ppermute only.
A program may use at most 64 MiB of HBM per device.

v0:
```python
import math

import jax
import jax.numpy as jnp
from jax import lax
from jax.sharding import PartitionSpec as P

RANK = 8
LEN = 256

TRADE = [(0, 1), (1, 0), (2, 3), (3, 2)]
TO_END = [(1, 0), (2, 3)]
ACROSS = [(1, 2), (2, 1)]
TO_MIDDLE = [(0, 1), (3, 2)]


def live_rows(seq_len, row_count):
    seq_count = seq_len.shape[0]
    seq_span = row_count // seq_count
    positions = lax.broadcasted_iota(jnp.int32, (seq_count, seq_span, 1), 1)
    live = (positions < seq_len[:, None, None]).astype(jnp.float32)
    return live.reshape(row_count, 1)


def column_scores(masked_acts, proj_grads, seq_count):
    product = masked_acts * proj_grads
    return jnp.sum(product.reshape(seq_count, -1, product.shape[1]), axis=1)


def rank_scores(columns):
    seq_count = columns.shape[0]
    return jnp.sum(columns.reshape(seq_count, -1, RANK), axis=2)


def dot(a, b):
    return jnp.dot(a, b, preferred_element_type=jnp.float32)


def on_any(acts, grads, left, right, seq_len):
    seq_count = seq_len.shape[0]
    live = live_rows(seq_len, acts.shape[0])
    proj_acts = dot(acts, lax.all_gather(left, "dp", axis=0, tiled=True))
    proj_grads = dot(grads, lax.all_gather(right, "dp", axis=0, tiled=True))
    masked = lax.psum(proj_acts, "mp") * live
    scores = rank_scores(column_scores(masked, proj_grads, seq_count))
    return lax.psum(scores, "mp") / math.sqrt(RANK * LEN)


def after(value, *arrived):
    return lax.optimization_barrier((value, *arrived))[0]


class Sender:
    def __init__(self, pairs):
        self.pairs = pairs
        self.came = []

    def ready(self, value, *arrived):
        return after(value, *self.came[-3:-1], *arrived)

    def __call__(self, x, pairs=None):
        self.came.append(lax.ppermute(x, "dp", pairs or self.pairs))
        return self.came[-1]


def on_line(acts, grads, left, right, seq_len):
    seq_count = seq_len.shape[0]
    row_count = acts.shape[0]
    place = lax.axis_index("dp")
    is_end = (place == 0) | (place == 3)
    near = place ^ 1
    far_middle = jnp.where(place < 2, 2, 1)
    far_end = jnp.where(place < 2, 3, 0)

    unit = left.shape[0]
    depth = right.shape[0]
    width = left.shape[1]
    kept = 3 * unit // 4
    spans = {"B": (0, kept), "C1": (kept, kept + unit), "C2": (kept + unit, kept + 2 * unit), "C3": (kept + 2 * unit, depth)}
    shares = [kept // 2, unit // 2, unit // 2, kept // 2, unit // 2, unit // 2]
    guests = [(kept + sum(shares[:i]), kept + sum(shares[: i + 1])) for i in range(len(shares))]
    trade = Sender(TRADE)
    across = Sender(ACROSS)

    def columns(array, source, start, stop):
        span = array.shape[1] // 4
        return lax.dynamic_slice_in_dim(array, source * span + start, stop - start, axis=1)

    def own(name, sender):
        start, stop = spans[name]
        return sender.ready(right)[start:stop]

    def guest(index, sender):
        source = sender.ready(grads)
        start, stop = guests[index]
        blocks = []
        while start < stop:
            block = columns(source, near, start, min(start + width, stop))
            start += width
            parts = width // block.shape[1]
            blocks.append(jnp.concatenate(jnp.split(block, parts, axis=0), axis=1))
        return jnp.concatenate(blocks, axis=0)

    def either(at_end, at_middle):
        return jnp.where(is_end, at_end, at_middle)

    x, y = {}, {}
    x["A"] = trade(left)
    y["AM"] = across(left)
    x["B"] = trade(right[:kept])
    y["AE"] = across(x["A"])
    x["AM"] = trade(either(own("C1", trade), y["AM"]))
    y["BM"] = across(own("B", across))
    x["AE"] = trade(either(own("C2", trade), y["AE"]))
    y["C1M"] = across(own("C1", across))
    x["BM"] = trade(either(guest(0, trade), y["BM"]))
    y["C2M"] = across(own("C2", across))
    x["C1M"] = trade(either(guest(1, trade), y["C1M"]))
    y["C3M"] = across(own("C3", across))
    x["C2M"] = trade(either(guest(2, trade), y["C2M"]))
    y["BE"] = across(across.ready(x["B"]))
    x["C3M"] = trade(either(own("C3", trade), y["C3M"]))
    y["C1E"] = across(across.ready(x["AM"]))
    x["BE"] = trade(either(guest(3, trade), y["BE"]))
    y["C2E"] = across(across.ready(x["AE"]))
    x["C1E"] = trade(either(guest(4, trade), y["C1E"]))
    y["C3E"] = across(after(x["C3M"], y["C2E"]))
    x["C2E"] = trade(either(guest(5, trade), y["C2E"]))
    x["C3E"] = trade(y["C3E"], TO_END)

    x["BM"] = after(x["BM"], x["AE"])
    x["AM"] = after(x["AM"], x["AE"])
    proj_acts = dot(columns(after(acts, x["A"], y["AM"]), place, 0, unit), left)
    proj_acts += dot(columns(acts, near, 0, unit), x["A"])
    proj_acts += dot(columns(acts, far_middle, 0, unit), either(x["AM"], y["AM"]))
    proj_acts += dot(columns(acts, far_end, 0, unit), either(x["AE"], y["AE"]))
    other_acts = lax.ppermute(proj_acts, "mp", [(0, 1), (1, 0)])
    masked = after((proj_acts + other_acts) * live_rows(seq_len, row_count))
    by_seq = masked.reshape(seq_count, -1, width)
    scale = jnp.maximum(jnp.max(jnp.abs(by_seq), axis=1, keepdims=True), 1e-30) / 32767
    coded = jnp.round(by_seq / scale).astype(jnp.int16).reshape(row_count, width)
    guest_acts = lax.ppermute(coded, "dp", TO_MIDDLE)

    def near_term(name, got):
        if name != "B":
            got = either(jnp.zeros_like(got), got)
        return dot(columns(grads, near, *spans[name]), got)

    def middle_term(name):
        return dot(columns(grads, far_middle, *spans[name]), either(x[name + "M"], y[name + "M"]))

    def end_term(name):
        return dot(columns(grads, far_end, *spans[name]), either(x[name + "E"], y[name + "E"]))

    def guest_term(index, got):
        start, stop = guests[index]
        total = None
        while start < stop:
            span = min(width, stop - start)
            rows = row_count * span // width
            block = jnp.concatenate(jnp.split(got[:rows], width // span, axis=1), axis=0)
            got = got[rows:]
            term = dot(block, right[start : start + span])
            total = term if total is None else total + term
            start += span
        return total

    proj_grads = dot(columns(after(grads, x["AE"]), place, 0, depth), right)
    proj_grads = after(proj_grads, x["AE"])
    proj_grads += near_term("B", after(x["B"], x["AM"], y["AE"]))
    proj_grads = after(proj_grads)
    proj_grads += near_term("C1", after(x["AM"], x["AE"]))
    proj_grads += near_term("C2", x["AE"])
    proj_grads = after(proj_grads)
    proj_grads += middle_term("B")
    guest_grads = guest_term(0, x["BM"])
    proj_grads += middle_term("C1")
    guest_grads += guest_term(1, x["C1M"])
    proj_grads, guest_grads = lax.optimization_barrier((proj_grads, guest_grads))
    proj_grads += middle_term("C2")
    guest_grads += guest_term(2, x["C2M"])
    proj_grads += middle_term("C3")
    proj_grads += near_term("C3", x["C3M"])
    proj_grads, guest_grads, masked = lax.optimization_barrier((proj_grads, guest_grads, masked))
    proj_grads += end_term("B")
    guest_grads += guest_term(3, x["BE"])
    proj_grads, guest_grads = lax.optimization_barrier((proj_grads, guest_grads))
    proj_grads += end_term("C1")
    guest_grads += guest_term(4, x["C1E"])
    proj_grads, guest_grads = lax.optimization_barrier((proj_grads, guest_grads))
    proj_grads += end_term("C2")
    guest_grads += guest_term(5, x["C2E"])
    guest_sums = column_scores(guest_acts.astype(jnp.float32), guest_grads, seq_count)
    guest_scores = lax.ppermute(guest_sums, "dp", TO_END) * scale[:, 0]

    proj_grads = after(proj_grads)
    proj_grads += end_term("C3")
    scores = rank_scores(column_scores(masked, proj_grads, seq_count) + guest_scores)
    other_scores = lax.ppermute(scores, "mp", [(0, 1), (1, 0)])
    return (scores + other_scores) / math.sqrt(RANK * LEN)


def suits_line(mesh, acts, left, right):
    unit, width = left.shape
    fits = right.shape[0] * 2 == unit * 7 and acts.shape[0] == 2 * width and unit == 4 * width
    return mesh.shape["dp"] == 4 and mesh.shape["mp"] == 2 and fits


def solution(mesh):
    def on_device(acts, grads, query_left, query_right, seq_len):
        body = on_line if suits_line(mesh, acts[0], query_left[0], query_right[0]) else on_any
        return body(acts[0], grads[0], query_left[0], query_right[0], seq_len)[None]

    return jax.shard_map(
        on_device,
        mesh=mesh,
        in_specs=(
            P("layer", ("groups", "dp"), "mp"),
            P("layer", ("groups", "dp"), "mp"),
            P("layer", ("mp", "dp"), "groups"),
            P("layer", ("mp", "dp"), "groups"),
            P(("groups", "dp")),
        ),
        out_specs=P("layer", ("groups", "dp"), None),
        check_vma=False,
    )
```

profile of v0, /device:TPU:0, one launch (start us, length us, event | category | flops | bytes accessed | tf_op | source)
XLA Modules:
  0.0 135.4 jit_solution(5233660918003416581)
XLA Ops:
  0.0 3.0 %collective-permute-start = (bf16[1024,256]{1,0:T(8,128)(2,1)}, bf16[1024,256]{1,0:T(8,128)(2,1)S(1)}, u32[]{:S(2)}, u32[]{:S(2)}) collective-permute-start(bf16[1024,256]{1,0:T(8,128)(2,1)} %bitcast.131), channel_id=1, source_target_pairs={{0,4},{4,0},{8,12},{12,8},{1,5},{5,1},{9,13},{13,9},{2,6},{6,2},{1... | collective-permute-start | bytes 1572872 | tf_op jit(solution)/shard_map/ppermute | solution.py:62
  3.0 0.7 collective-permute-start.4
  3.7 1.8 %slice_bitcast_fusion = bf16[768,256]{1,0:T(8,128)(2,1)} fusion(bf16[1,3584,256]{2,1,0:T(8,128)(2,1)} %param.8), kind=kLoop, calls=%fused_computation.101 | loop fusion | bytes 786432 | tf_op jit(solution)/shard_map/slice | solution.py:110
  5.5 4.4 %collective-permute-start.1 = (bf16[768,256]{1,0:T(8,128)(2,1)}, bf16[768,256]{1,0:T(8,128)(2,1)}, u32[]{:S(2)}, u32[]{:S(2)}) collective-permute-start(bf16[768,256]{1,0:T(8,128)(2,1)} %slice_bitcast_fusion), channel_id=1, source_target_pairs={{0,4},{4,0},{8,12},{12,8},{1,5},{5,1},{9,13},{13,9},{2,6},{6,2},{1... | collective-permute-start | bytes 1179656 | tf_op jit(solution)/shard_map/ppermute | solution.py:62
  9.9 6.1 %collective-permute-done = bf16[1024,256]{1,0:T(8,128)(2,1)S(1)} collective-permute-done((bf16[1024,256]{1,0:T(8,128)(2,1)}, bf16[1024,256]{1,0:T(8,128)(2,1)S(1)}, u32[]{:S(2)}, u32[]{:S(2)}) %collective-permute-start) | collective-permute-done | bytes 524320 | tf_op jit(solution)/shard_map/ppermute | solution.py:62
  16.0 0.7 collective-permute-start.2
  16.7 0.7 fusion.151
  17.4 1.1 slice.139
  18.5 0.7 collective-permute-start.6
  19.2 1.3 slice_select_fusion
  20.5 6.6 %collective-permute-start.5 = (bf16[1024,256]{1,0:T(8,128)(2,1)S(1)}, bf16[1024,256]{1,0:T(8,128)(2,1)S(1)}, u32[]{:S(2)}, u32[]{:S(2)}) collective-permute-start(bf16[1024,256]{1,0:T(8,128)(2,1)S(1)} %slice_select_fusion), channel_id=1, source_target_pairs={{0,4},{4,0},{8,12},{12,8},{1,5},{5,1},{9,13},{13,9},{2,6},{6,2},{1... | collective-permute-start | bytes 1572872 | tf_op jit(solution)/shard_map/ppermute | solution.py:62
  27.1 1.7 %fusion.14 = f32[512,256]{1,0:T(8,128)S(1)} fusion(bf16[1024,256]{1,0:T(8,128)(2,1)S(1)} %collective-permute-done, bf16[1,512,4096]{2,1,0:T(8,128)(2,1)} %param.5, s32[]{:T(128)S(6)} %select_n.217), kind=kOutput, calls=%fused_computation.29 | convolution fusion | flops 268435456 | bytes 2097156 | tf_op jit(solution)/shard_map/dot_general | solution.py:36
  28.8 0.7 collective-permute-start.8
  29.6 8.9 %collective-permute-start.3 = (bf16[1024,256]{1,0:T(8,128)(2,1)S(1)}, bf16[1024,256]{1,0:T(8,128)(2,1)S(1)}, u32[]{:S(2)}, u32[]{:S(2)}) collective-permute-start(bf16[1024,256]{1,0:T(8,128)(2,1)S(1)} %slice_select_fusion.1), channel_id=1, source_target_pairs={{0,4},{4,0},{8,12},{12,8},{1,5},{5,1},{9,13},{13,9},{2,6},{6,2},{1... | collective-permute-start | bytes 1572872 | tf_op jit(solution)/shard_map/ppermute | solution.py:62
  38.5 1.7 %convolution_add_fusion.6 = f32[512,256]{1,0:T(8,128)S(1)} fusion(f32[512,256]{1,0:T(8,128)S(1)} %fusion.14, bf16[512,4096]{1,0:T(8,128)(2,1)} %bitcast.130, s32[]{:T(128)S(6)} %select_n.216, bf16[1,1024,256]{2,1,0:T(8,128)(2,1)S(1)} %copy-done.3), kind=kOutput, calls=%fused_computation.8 | convolution fusion | flops 268566528 | bytes 2621444 | tf_op jit(solution)/shard_map/dot_general | solution.py:36
  40.2 0.9 constant_dynamic-slice_fusion
  41.0 1.0 constant_dynamic-slice_fusion.11
  42.2 1.8 %collective-permute-start.7 = (bf16[768,256]{1,0:T(8,128)(2,1)S(1)}, bf16[768,256]{1,0:T(8,128)(2,1)S(1)}, u32[]{:S(2)}, u32[]{:S(2)}) collective-permute-start(bf16[768,256]{1,0:T(8,128)(2,1)S(1)} %maximum_select_fusion.4), channel_id=1, source_target_pairs={{0,4},{4,0},{8,12},{12,8},{1,5},{5,1},{9,13},{13,9},{2,6},{6,2},{1... | collective-permute-start | bytes 1179656 | tf_op jit(solution)/shard_map/ppermute | solution.py:62
  44.0 0.7 collective-permute-start.10
  44.8 0.7 collective-permute-start.12
  45.5 5.8 %collective-permute-done.3 = bf16[1024,256]{1,0:T(8,128)(2,1)S(1)} collective-permute-done((bf16[1024,256]{1,0:T(8,128)(2,1)S(1)}, bf16[1024,256]{1,0:T(8,128)(2,1)S(1)}, u32[]{:S(2)}, u32[]{:S(2)}) %collective-permute-start.3) | collective-permute-done | bytes 524320 | tf_op jit(solution)/shard_map/ppermute | solution.py:62
  51.3 1.1 constant_dynamic-slice_fusion.10
  52.5 6.8 %collective-permute-start.9 = (bf16[1024,256]{1,0:T(8,128)(2,1)S(1)}, bf16[1024,256]{1,0:T(8,128)(2,1)S(1)}, u32[]{:S(2)}, u32[]{:S(2)}) collective-permute-start(bf16[1024,256]{1,0:T(8,128)(2,1)S(1)} %maximum_select_fusion), channel_id=1, source_target_pairs={{0,4},{4,0},{8,12},{12,8},{1,5},{5,1},{9,13},{13,9},{2,6},{6,2},{1... | collective-permute-start | bytes 1572872 | tf_op jit(solution)/shard_map/ppermute | solution.py:62
  59.3 1.1 fusion
  60.7 1.5 %convolution_add_fusion.2 = f32[512,256]{1,0:T(8,128)S(1)} fusion(f32[512,256]{1,0:T(8,128)S(1)} %fusion, bf16[768,256]{1,0:T(8,128)(2,1)} %collective-permute-done.1, bf16[1,512,14336]{2,1,0:T(8,128)(2,1)S(1)} %copy-done.1, s32[]{:T(128)S(6)} %select_n.189), kind=kOutput, calls=%fused_computation.4 | convolution fusion | flops 201457664 | bytes 2228228 | tf_op jit(solution)/shard_map/dot_general | solution.py:36
  62.3 0.4 fusion.20
  62.7 0.2 convolution_add_fusion.14
  63.1 2.8 %collective-permute-start.11 = (bf16[1024,256]{1,0:T(8,128)(2,1)S(1)}, bf16[1024,256]{1,0:T(8,128)(2,1)S(1)}, u32[]{:S(2)}, u32[]{:S(2)}) collective-permute-start(bf16[1024,256]{1,0:T(8,128)(2,1)S(1)} %maximum_select_fusion.1), channel_id=1, source_target_pairs={{0,4},{4,0},{8,12},{12,8},{1,5},{5,1},{9,13},{13,9},{2,6},{6,2},{1... | collective-permute-start | bytes 1572872 | tf_op jit(solution)/shard_map/ppermute | solution.py:62
  65.9 0.5 convolution_add_fusion.5
  66.4 0.5 convolution_add_fusion.4
  66.8 1.6 %collective-permute-start.14 = (f32[512,256]{1,0:T(8,128)S(1)}, f32[512,256]{1,0:T(8,128)S(1)}, u32[]{:S(2)}, u32[]{:S(2)}) collective-permute-start(f32[512,256]{1,0:T(8,128)S(1)} %convolution_add_fusion.4), channel_id=1, source_target_pairs={{0,2},{2,0},{1,3},{3,1},{4,6},{6,4},{5,7},{7,5},{8,10},{10,8},{9,1... | collective-permute-start | bytes 1572872 | tf_op jit(solution)/shard_map/ppermute | solution.py:137
  68.4 0.7 collective-permute-start.15
  69.1 0.5 convolution_add_fusion.8
  69.5 0.4 fusion.38
  69.9 0.7 collective-permute-start.17
  70.6 0.7 collective-permute-start.19
  71.3 0.8 collective-permute-done.9
  72.2 14.0 %collective-permute-start.13 = (bf16[768,256]{1,0:T(8,128)(2,1)S(1)}, bf16[768,256]{1,0:T(8,128)(2,1)S(1)}, u32[]{:S(2)}, u32[]{:S(2)}) collective-permute-start(bf16[768,256]{1,0:T(8,128)(2,1)S(1)} %slice_select_fusion.2), channel_id=1, source_target_pairs={{0,4},{4,0},{8,12},{12,8},{1,5},{5,1},{9,13},{13,9},{2,6},{6,2},{1... | collective-permute-start | bytes 1179656 | tf_op jit(solution)/shard_map/ppermute | solution.py:62
  86.8 3.9 %collective-permute-start.23 = (s16[512,256]{1,0:T(8,128)(2,1)S(1)}, s16[512,256]{1,0:T(8,128)(2,1)S(1)}, u32[]{:S(2)}, u32[]{:S(2)}) collective-permute-start(s16[512,256]{1,0:T(8,128)(2,1)S(1)} %fusion.48), channel_id=1, source_target_pairs={{0,4},{12,8},{1,5},{13,9},{2,6},{14,10},{3,7},{15,11},{16,20},{28,... | collective-permute-start | bytes 786440 | tf_op jit(solution)/shard_map/ppermute | solution.py:142
  91.2 0.5 add_add_fusion
  91.9 0.2 fusion.6
  92.1 4.1 %collective-permute-done.13 = bf16[768,256]{1,0:T(8,128)(2,1)S(1)} collective-permute-done((bf16[768,256]{1,0:T(8,128)(2,1)S(1)}, bf16[768,256]{1,0:T(8,128)(2,1)S(1)}, u32[]{:S(2)}, u32[]{:S(2)}) %collective-permute-start.13) | collective-permute-done | bytes 393248 | tf_op jit(solution)/shard_map/ppermute | solution.py:62
  96.2 0.4 fusion.36
  96.6 0.4 fusion.34
  97.0 0.5 fusion.8
  97.7 2.1 %collective-permute-start.18 = (bf16[1024,256]{1,0:T(8,128)(2,1)S(1)}, bf16[1024,256]{1,0:T(8,128)(2,1)S(1)}, u32[]{:S(2)}, u32[]{:S(2)}) collective-permute-start(bf16[1024,256]{1,0:T(8,128)(2,1)S(1)} %maximum_select_fusion.2), channel_id=1, source_target_pairs={{0,4},{4,0},{8,12},{12,8},{1,5},{5,1},{9,13},{13,9},{2,6},{6,2},{1... | collective-permute-start | bytes 1572872 | tf_op jit(solution)/shard_map/ppermute | solution.py:62
  99.8 0.7 collective-permute-start.21
  100.4 3.7 %collective-permute-done.16 = bf16[768,256]{1,0:T(8,128)(2,1)S(1)} collective-permute-done((bf16[768,256]{1,0:T(8,128)(2,1)S(1)}, bf16[768,256]{1,0:T(8,128)(2,1)S(1)}, u32[]{:S(2)}, u32[]{:S(2)}) %collective-permute-start.16) | collective-permute-done | bytes 393248 | tf_op jit(solution)/shard_map/ppermute | solution.py:62
  104.4 0.2 fusion.5
  104.6 0.4 convolution_add_fusion.1
  105.2 2.5 %collective-permute-start.20 = (bf16[1024,256]{1,0:T(8,128)(2,1)S(1)}, bf16[1024,256]{1,0:T(8,128)(2,1)S(1)}, u32[]{:S(2)}, u32[]{:S(2)}) collective-permute-start(bf16[1024,256]{1,0:T(8,128)(2,1)S(1)} %maximum_select_fusion.3), channel_id=1, source_target_pairs={{0,4},{4,0},{8,12},{12,8},{1,5},{5,1},{9,13},{13,9},{2,6},{6,2},{1... | collective-permute-start | bytes 1572872 | tf_op jit(solution)/shard_map/ppermute | solution.py:62
  107.8 1.3 collective-permute-start.22
  109.1 9.9 %collective-permute-done.18 = bf16[1024,256]{1,0:T(8,128)(2,1)S(1)} collective-permute-done((bf16[1024,256]{1,0:T(8,128)(2,1)S(1)}, bf16[1024,256]{1,0:T(8,128)(2,1)S(1)}, u32[]{:S(2)}, u32[]{:S(2)}) %collective-permute-start.18) | collective-permute-done | bytes 524320 | tf_op jit(solution)/shard_map/ppermute | solution.py:62
  119.0 0.5 fusion.10
  120.1 4.5 %collective-permute-done.20 = bf16[1024,256]{1,0:T(8,128)(2,1)S(1)} collective-permute-done((bf16[1024,256]{1,0:T(8,128)(2,1)S(1)}, bf16[1024,256]{1,0:T(8,128)(2,1)S(1)}, u32[]{:S(2)}, u32[]{:S(2)}) %collective-permute-start.20) | collective-permute-done | bytes 524320 | tf_op jit(solution)/shard_map/ppermute | solution.py:62
  124.6 0.5 convolution_add_fusion.3
  125.3 0.2 bitcast_reduce_fusion
  125.6 1.3 collective-permute-start.24
  126.9 1.3 collective-permute-done.22
  128.2 0.4 bitcast_reduce_fusion.2
  128.6 2.4 %collective-permute-done.24 = f32[2,256]{1,0:T(2,128)S(1)} collective-permute-done((f32[2,256]{1,0:T(2,128)S(1)}, f32[2,256]{1,0:T(2,128)S(1)}, u32[]{:S(2)}, u32[]{:S(2)}) %collective-permute-start.24) | collective-permute-done | bytes 2080 | tf_op jit(solution)/shard_map/ppermute | solution.py:194
  131.2 1.5 %collective-permute-start.25 = (f32[2,32]{1,0:T(2,128)S(1)}, f32[2,32]{1,0:T(2,128)S(1)}, u32[]{:S(2)}, u32[]{:S(2)}) collective-permute-start(f32[2,32]{1,0:T(2,128)S(1)} %reduce_sum.29), channel_id=1, source_target_pairs={{0,2},{2,0},{1,3},{3,1},{4,6},{6,4},{5,7},{7,5},{8,10},{10,8},{9,1... | collective-permute-start | bytes 776 | tf_op jit(solution)/shard_map/ppermute | solution.py:199
  132.7 2.1 %collective-permute-done.25 = f32[2,32]{1,0:T(2,128)S(1)} collective-permute-done((f32[2,32]{1,0:T(2,128)S(1)}, f32[2,32]{1,0:T(2,128)S(1)}, u32[]{:S(2)}, u32[]{:S(2)}) %collective-permute-start.25) | collective-permute-done | bytes 288 | tf_op jit(solution)/shard_map/ppermute | solution.py:199
  134.8 0.6 multiply_bitcast_fusion
  (61 shorter events, 3.8 us)
Async XLA Ops:
  0.0 28.7 %copy-start = (bf16[1,3584,256]{2,1,0:T(8,128)(2,1)S(1)}, bf16[1,3584,256]{2,1,0:T(8,128)(2,1)}, u32[]{:S(2)}) copy-start(bf16[1,3584,256]{2,1,0:T(8,128)(2,1)} %param.8) | copy-start | bytes 5505028
  0.0 16.0 %collective-permute-start = (bf16[1024,256]{1,0:T(8,128)(2,1)}, bf16[1024,256]{1,0:T(8,128)(2,1)S(1)}, u32[]{:S(2)}, u32[]{:S(2)}) collective-permute-start(bf16[1024,256]{1,0:T(8,128)(2,1)} %bitcast.131), channel_id=1, source_target_pairs={{0,4},{4,0},{8,12},{12,8},{1,5},{5,1},{9,13},{13,9},{2,6},{6,2},{1... | collective-permute-start | bytes 1572872 | tf_op jit(solution)/shard_map/ppermute | solution.py:62
  3.0 14.4 %collective-permute-start.4 = (bf16[1024,256]{1,0:T(8,128)(2,1)}, bf16[1024,256]{1,0:T(8,128)(2,1)S(1)}, u32[]{:S(2)}, u32[]{:S(2)}) collective-permute-start(bf16[1024,256]{1,0:T(8,128)(2,1)} %bitcast.132), channel_id=1, source_target_pairs={{4,8},{8,4},{5,9},{9,5},{6,10},{10,6},{7,11},{11,7},{20,24},{24,20... | collective-permute-start | bytes 1572872 | tf_op jit(solution)/shard_map/ppermute | solution.py:62
  5.5 21.6 %collective-permute-start.1 = (bf16[768,256]{1,0:T(8,128)(2,1)}, bf16[768,256]{1,0:T(8,128)(2,1)}, u32[]{:S(2)}, u32[]{:S(2)}) collective-permute-start(bf16[768,256]{1,0:T(8,128)(2,1)} %slice_bitcast_fusion), channel_id=1, source_target_pairs={{0,4},{4,0},{8,12},{12,8},{1,5},{5,1},{9,13},{13,9},{2,6},{6,2},{1... | collective-permute-start | bytes 1179656 | tf_op jit(solution)/shard_map/ppermute | solution.py:62
  16.0 12.7 %collective-permute-start.2 = (bf16[1024,256]{1,0:T(8,128)(2,1)S(1)}, bf16[1024,256]{1,0:T(8,128)(2,1)S(1)}, u32[]{:S(2)}, u32[]{:S(2)}) collective-permute-start(bf16[1024,256]{1,0:T(8,128)(2,1)S(1)} %collective-permute-done), channel_id=1, source_target_pairs={{4,8},{8,4},{5,9},{9,5},{6,10},{10,6},{7,11},{11,7},{20,24},{24,20... | collective-permute-start | bytes 1572872 | tf_op jit(solution)/shard_map/ppermute | solution.py:62
  17.4 21.0 %copy-start.3 = (bf16[1,1024,256]{2,1,0:T(8,128)(2,1)S(1)}, bf16[1,1024,256]{2,1,0:T(8,128)(2,1)}, u32[]{:S(2)}) copy-start(bf16[1,1024,256]{2,1,0:T(8,128)(2,1)} %param.7) | copy-start | bytes 1572868
  18.5 23.5 %collective-permute-start.6 = (bf16[768,256]{1,0:T(8,128)(2,1)S(1)}, bf16[768,256]{1,0:T(8,128)(2,1)S(1)}, u32[]{:S(2)}, u32[]{:S(2)}) collective-permute-start(bf16[768,256]{1,0:T(8,128)(2,1)S(1)} %slice.139), channel_id=1, source_target_pairs={{4,8},{8,4},{5,9},{9,5},{6,10},{10,6},{7,11},{11,7},{20,24},{24,20... | collective-permute-start | bytes 1179656 | tf_op jit(solution)/shard_map/ppermute | solution.py:62
  19.2 40.1 %copy-start.1 = (bf16[1,512,14336]{2,1,0:T(8,128)(2,1)S(1)}, bf16[1,512,14336]{2,1,0:T(8,128)(2,1)}, u32[]{:S(2)}) copy-start(bf16[1,512,14336]{2,1,0:T(8,128)(2,1)} %param.6) | copy-start | bytes 44040196
  20.5 19.7 %collective-permute-start.5 = (bf16[1024,256]{1,0:T(8,128)(2,1)S(1)}, bf16[1024,256]{1,0:T(8,128)(2,1)S(1)}, u32[]{:S(2)}, u32[]{:S(2)}) collective-permute-start(bf16[1024,256]{1,0:T(8,128)(2,1)S(1)} %slice_select_fusion), channel_id=1, source_target_pairs={{0,4},{4,0},{8,12},{12,8},{1,5},{5,1},{9,13},{13,9},{2,6},{6,2},{1... | collective-permute-start | bytes 1572872 | tf_op jit(solution)/shard_map/ppermute | solution.py:62
  28.8 15.9 %collective-permute-start.8 = (bf16[1024,256]{1,0:T(8,128)(2,1)S(1)}, bf16[1024,256]{1,0:T(8,128)(2,1)S(1)}, u32[]{:S(2)}, u32[]{:S(2)}) collective-permute-start(bf16[1024,256]{1,0:T(8,128)(2,1)S(1)} %slice.140), channel_id=1, source_target_pairs={{4,8},{8,4},{5,9},{9,5},{6,10},{10,6},{7,11},{11,7},{20,24},{24,20... | collective-permute-start | bytes 1572872 | tf_op jit(solution)/shard_map/ppermute | solution.py:62
  29.6 21.7 %collective-permute-start.3 = (bf16[1024,256]{1,0:T(8,128)(2,1)S(1)}, bf16[1024,256]{1,0:T(8,128)(2,1)S(1)}, u32[]{:S(2)}, u32[]{:S(2)}) collective-permute-start(bf16[1024,256]{1,0:T(8,128)(2,1)S(1)} %slice_select_fusion.1), channel_id=1, source_target_pairs={{0,4},{4,0},{8,12},{12,8},{1,5},{5,1},{9,13},{13,9},{2,6},{6,2},{1... | collective-permute-start | bytes 1572872 | tf_op jit(solution)/shard_map/ppermute | solution.py:62
  42.2 18.3 %collective-permute-start.7 = (bf16[768,256]{1,0:T(8,128)(2,1)S(1)}, bf16[768,256]{1,0:T(8,128)(2,1)S(1)}, u32[]{:S(2)}, u32[]{:S(2)}) collective-permute-start(bf16[768,256]{1,0:T(8,128)(2,1)S(1)} %maximum_select_fusion.4), channel_id=1, source_target_pairs={{0,4},{4,0},{8,12},{12,8},{1,5},{5,1},{9,13},{13,9},{2,6},{6,2},{1... | collective-permute-start | bytes 1179656 | tf_op jit(solution)/shard_map/ppermute | solution.py:62
  44.0 19.0 %collective-permute-start.10 = (bf16[1024,256]{1,0:T(8,128)(2,1)S(1)}, bf16[1024,256]{1,0:T(8,128)(2,1)S(1)}, u32[]{:S(2)}, u32[]{:S(2)}) collective-permute-start(bf16[1024,256]{1,0:T(8,128)(2,1)S(1)} %slice.152), channel_id=1, source_target_pairs={{4,8},{8,4},{5,9},{9,5},{6,10},{10,6},{7,11},{11,7},{20,24},{24,20... | collective-permute-start | bytes 1572872 | tf_op jit(solution)/shard_map/ppermute | solution.py:62
  44.8 25.2 %collective-permute-start.12 = (bf16[768,256]{1,0:T(8,128)(2,1)S(1)}, bf16[768,256]{1,0:T(8,128)(2,1)S(1)}, u32[]{:S(2)}, u32[]{:S(2)}) collective-permute-start(bf16[768,256]{1,0:T(8,128)(2,1)S(1)} %slice.154), channel_id=1, source_target_pairs={{4,8},{8,4},{5,9},{9,5},{6,10},{10,6},{7,11},{11,7},{20,24},{24,20... | collective-permute-start | bytes 1179656 | tf_op jit(solution)/shard_map/ppermute | solution.py:62
  52.5 19.6 %collective-permute-start.9 = (bf16[1024,256]{1,0:T(8,128)(2,1)S(1)}, bf16[1024,256]{1,0:T(8,128)(2,1)S(1)}, u32[]{:S(2)}, u32[]{:S(2)}) collective-permute-start(bf16[1024,256]{1,0:T(8,128)(2,1)S(1)} %maximum_select_fusion), channel_id=1, source_target_pairs={{0,4},{4,0},{8,12},{12,8},{1,5},{5,1},{9,13},{13,9},{2,6},{6,2},{1... | collective-permute-start | bytes 1572872 | tf_op jit(solution)/shard_map/ppermute | solution.py:62
  60.7 5.2 %copy-start.2 = (bf16[1,512,4096]{2,1,0:T(8,128)(2,1)S(1)}, bf16[1,512,4096]{2,1,0:T(8,128)(2,1)}, u32[]{:S(2)}) copy-start(bf16[1,512,4096]{2,1,0:T(8,128)(2,1)} %param.5) | copy-start | bytes 12582916
  63.1 23.2 %collective-permute-start.11 = (bf16[1024,256]{1,0:T(8,128)(2,1)S(1)}, bf16[1024,256]{1,0:T(8,128)(2,1)S(1)}, u32[]{:S(2)}, u32[]{:S(2)}) collective-permute-start(bf16[1024,256]{1,0:T(8,128)(2,1)S(1)} %maximum_select_fusion.1), channel_id=1, source_target_pairs={{0,4},{4,0},{8,12},{12,8},{1,5},{5,1},{9,13},{13,9},{2,6},{6,2},{1... | collective-permute-start | bytes 1572872 | tf_op jit(solution)/shard_map/ppermute | solution.py:62
  66.8 19.3 %collective-permute-start.14 = (f32[512,256]{1,0:T(8,128)S(1)}, f32[512,256]{1,0:T(8,128)S(1)}, u32[]{:S(2)}, u32[]{:S(2)}) collective-permute-start(f32[512,256]{1,0:T(8,128)S(1)} %convolution_add_fusion.4), channel_id=1, source_target_pairs={{0,2},{2,0},{1,3},{3,1},{4,6},{6,4},{5,7},{7,5},{8,10},{10,8},{9,1... | collective-permute-start | bytes 1572872 | tf_op jit(solution)/shard_map/ppermute | solution.py:137
  68.4 2.2 %collective-permute-start.15 = (bf16[768,256]{1,0:T(8,128)(2,1)}, bf16[768,256]{1,0:T(8,128)(2,1)S(1)}, u32[]{:S(2)}, u32[]{:S(2)}) collective-permute-start(bf16[768,256]{1,0:T(8,128)(2,1)} %collective-permute-done.1), channel_id=1, source_target_pairs={{4,8},{8,4},{5,9},{9,5},{6,10},{10,6},{7,11},{11,7},{20,24},{24,20... | collective-permute-start | bytes 1179656 | tf_op jit(solution)/shard_map/ppermute | solution.py:62
  69.9 27.6 %collective-permute-start.17 = (bf16[1024,256]{1,0:T(8,128)(2,1)S(1)}, bf16[1024,256]{1,0:T(8,128)(2,1)S(1)}, u32[]{:S(2)}, u32[]{:S(2)}) collective-permute-start(bf16[1024,256]{1,0:T(8,128)(2,1)S(1)} %collective-permute-done.5), channel_id=1, source_target_pairs={{4,8},{8,4},{5,9},{9,5},{6,10},{10,6},{7,11},{11,7},{20,24},{24,20... | collective-permute-start | bytes 1572872 | tf_op jit(solution)/shard_map/ppermute | solution.py:62
  70.6 29.1 %collective-permute-start.19 = (bf16[1024,256]{1,0:T(8,128)(2,1)S(1)}, bf16[1024,256]{1,0:T(8,128)(2,1)S(1)}, u32[]{:S(2)}, u32[]{:S(2)}) collective-permute-start(bf16[1024,256]{1,0:T(8,128)(2,1)S(1)} %collective-permute-done.3), channel_id=1, source_target_pairs={{4,8},{8,4},{5,9},{9,5},{6,10},{10,6},{7,11},{11,7},{20,24},{24,20... | collective-permute-start | bytes 1572872 | tf_op jit(solution)/shard_map/ppermute | solution.py:62
  72.2 24.0 %collective-permute-start.13 = (bf16[768,256]{1,0:T(8,128)(2,1)S(1)}, bf16[768,256]{1,0:T(8,128)(2,1)S(1)}, u32[]{:S(2)}, u32[]{:S(2)}) collective-permute-start(bf16[768,256]{1,0:T(8,128)(2,1)S(1)} %slice_select_fusion.2), channel_id=1, source_target_pairs={{0,4},{4,0},{8,12},{12,8},{1,5},{5,1},{9,13},{13,9},{2,6},{6,2},{1... | collective-permute-start | bytes 1179656 | tf_op jit(solution)/shard_map/ppermute | solution.py:62
  86.6 17.6 %collective-permute-start.16 = (bf16[768,256]{1,0:T(8,128)(2,1)S(1)}, bf16[768,256]{1,0:T(8,128)(2,1)S(1)}, u32[]{:S(2)}, u32[]{:S(2)}) collective-permute-start(bf16[768,256]{1,0:T(8,128)(2,1)S(1)} %maximum_select_fusion.5), channel_id=1, source_target_pairs={{0,4},{4,0},{8,12},{12,8},{1,5},{5,1},{9,13},{13,9},{2,6},{6,2},{1... | collective-permute-start | bytes 1179656 | tf_op jit(solution)/shard_map/ppermute | solution.py:62
  86.8 38.5 %collective-permute-start.23 = (s16[512,256]{1,0:T(8,128)(2,1)S(1)}, s16[512,256]{1,0:T(8,128)(2,1)S(1)}, u32[]{:S(2)}, u32[]{:S(2)}) collective-permute-start(s16[512,256]{1,0:T(8,128)(2,1)S(1)} %fusion.48), channel_id=1, source_target_pairs={{0,4},{12,8},{1,5},{13,9},{2,6},{14,10},{3,7},{15,11},{16,20},{28,... | collective-permute-start | bytes 786440 | tf_op jit(solution)/shard_map/ppermute | solution.py:142
  97.7 21.3 %collective-permute-start.18 = (bf16[1024,256]{1,0:T(8,128)(2,1)S(1)}, bf16[1024,256]{1,0:T(8,128)(2,1)S(1)}, u32[]{:S(2)}, u32[]{:S(2)}) collective-permute-start(bf16[1024,256]{1,0:T(8,128)(2,1)S(1)} %maximum_select_fusion.2), channel_id=1, source_target_pairs={{0,4},{4,0},{8,12},{12,8},{1,5},{5,1},{9,13},{13,9},{2,6},{6,2},{1... | collective-permute-start | bytes 1572872 | tf_op jit(solution)/shard_map/ppermute | solution.py:62
  99.8 8.0 %collective-permute-start.21 = (bf16[768,256]{1,0:T(8,128)(2,1)S(1)}, bf16[768,256]{1,0:T(8,128)(2,1)S(1)}, u32[]{:S(2)}, u32[]{:S(2)}) collective-permute-start(bf16[768,256]{1,0:T(8,128)(2,1)S(1)} %collective-permute-done.13), channel_id=1, source_target_pairs={{4,8},{8,4},{5,9},{9,5},{6,10},{10,6},{7,11},{11,7},{20,24},{24,20... | collective-permute-start | bytes 1179656 | tf_op jit(solution)/shard_map/ppermute | solution.py:62
  105.2 19.4 %collective-permute-start.20 = (bf16[1024,256]{1,0:T(8,128)(2,1)S(1)}, bf16[1024,256]{1,0:T(8,128)(2,1)S(1)}, u32[]{:S(2)}, u32[]{:S(2)}) collective-permute-start(bf16[1024,256]{1,0:T(8,128)(2,1)S(1)} %maximum_select_fusion.3), channel_id=1, source_target_pairs={{0,4},{4,0},{8,12},{12,8},{1,5},{5,1},{9,13},{13,9},{2,6},{6,2},{1... | collective-permute-start | bytes 1572872 | tf_op jit(solution)/shard_map/ppermute | solution.py:62
  107.8 20.4 %collective-permute-start.22 = (bf16[768,256]{1,0:T(8,128)(2,1)S(1)}, bf16[768,256]{1,0:T(8,128)(2,1)S(1)}, u32[]{:S(2)}, u32[]{:S(2)}) collective-permute-start(bf16[768,256]{1,0:T(8,128)(2,1)S(1)} %collective-permute-done.21), channel_id=1, source_target_pairs={{4,0},{8,12},{5,1},{9,13},{6,2},{10,14},{7,3},{11,15},{20,16},{24,... | collective-permute-start | bytes 1179656 | tf_op jit(solution)/shard_map/ppermute | solution.py:62
  125.6 5.5 %collective-permute-start.24 = (f32[2,256]{1,0:T(2,128)S(1)}, f32[2,256]{1,0:T(2,128)S(1)}, u32[]{:S(2)}, u32[]{:S(2)}) collective-permute-start(f32[2,256]{1,0:T(2,128)S(1)} %bitcast_reduce_fusion), channel_id=1, source_target_pairs={{4,0},{8,12},{5,1},{9,13},{6,2},{10,14},{7,3},{11,15},{20,16},{24,... | collective-permute-start | bytes 6152 | tf_op jit(solution)/shard_map/ppermute | solution.py:194
  131.2 3.6 %collective-permute-start.25 = (f32[2,32]{1,0:T(2,128)S(1)}, f32[2,32]{1,0:T(2,128)S(1)}, u32[]{:S(2)}, u32[]{:S(2)}) collective-permute-start(f32[2,32]{1,0:T(2,128)S(1)} %reduce_sum.29), channel_id=1, source_target_pairs={{0,2},{2,0},{1,3},{3,1},{4,6},{6,4},{5,7},{7,5},{8,10},{10,8},{9,1... | collective-permute-start | bytes 776 | tf_op jit(solution)/shard_map/ppermute | solution.py:199
where the time goes:
time: 136 us; the launch traced here: 135 us
  starting transfers between devices  69.3 us (51%)
  waiting for transfers between devices  40.9 us (30%)
  matrix products  14.3 us (11%)
  local copies, waits for them, and re-layouts  6.34 us (5%)
  other arithmetic  3.94 us (3%)
    ppermute x22, starting transfers between devices, __call__(): self.came.append(lax.ppermute(x, 'dp', pairs or self.pairs))  61 us
    ppermute x22, waiting for transfers between devices, __call__(): self.came.append(lax.ppermute(x, 'dp', pairs or self.pairs))  36.3 us
    dot_general x29, matrix products, dot(): return jnp.dot(a, b, preferred_element_type=jnp.float32)  14.3 us
    ppermute x1, starting transfers between devices, on_line(): guest_acts = lax.ppermute(coded, 'dp', TO_MIDDLE)  3.92 us
  transfers between devices with their start and end apart: 26, of which 10 were waited for; matrix products, arithmetic and copies ran while one was open for 18% of the time, Pallas kernels for 0%

commit v1 on v0

--- a/solution.py
+++ b/solution.py
@@ -126,7 +126,7 @@
     x["C1E"] = trade(either(guest(4, trade), y["C1E"]))
     y["C3E"] = across(after(x["C3M"], y["C2E"]))
     x["C2E"] = trade(either(guest(5, trade), y["C2E"]))
-    x["C3E"] = trade(y["C3E"], TO_END)
+    x["C3E"] = trade(after(y["C3E"], x["C1E"]), TO_END)
 
     x["BM"] = after(x["BM"], x["AE"])
     x["AM"] = after(x["AM"], x["AE"])
@@ -188,13 +188,12 @@
     proj_grads += end_term("C1")
     guest_grads += guest_term(4, x["C1E"])
     proj_grads, guest_grads = lax.optimization_barrier((proj_grads, guest_grads))
-    proj_grads += end_term("C2")
     guest_grads += guest_term(5, x["C2E"])
     guest_sums = column_scores(guest_acts.astype(jnp.float32), guest_grads, seq_count)
     guest_scores = lax.ppermute(guest_sums, "dp", TO_END) * scale[:, 0]
 
     proj_grads = after(proj_grads)
-    proj_grads += end_term("C3")
+    proj_grads += end_term("C2") + end_term("C3")
     scores = rank_scores(column_scores(masked, proj_grads, seq_count) + guest_scores)
     other_scores = lax.ppermute(scores, "mp", [(0, 1), (1, 0)])
     return (scores + other_scores) / math.sqrt(RANK * LEN)

time: 136 us -> 136 us (level)
  waiting for transfers between devices: 40.9 us -> 38.7 us
  starting transfers between devices: 69.3 us -> 71 us
    ppermute x1, waiting for transfers between devices: 2.44 us -> 0.01 us  [on_line(): guest_scores = lax.ppermute(guest_sums, 'dp', TO_END) * scale[:, 0]]
    ppermute x22, starting transfers between devices: 61 us -> 62.7 us  [__call__(): self.came.append(lax.ppermute(x, 'dp', pairs or self.pairs))]
  transfers between devices with their start and end apart: 26 -> 26, of which waited for: 10 -> 9; matrix products, arithmetic and copies ran while one was open for 18% -> 18% of each run, Pallas kernels for 0% -> 0%
where the time goes in v1:
time: 136 us; the launch traced here: 135 us
  starting transfers between devices  71 us (52%)
  waiting for transfers between devices  38.7 us (28%)
  matrix products  14.3 us (11%)
  local copies, waits for them, and re-layouts  6.34 us (5%)
  other arithmetic  4.02 us (3%)
    ppermute x22, starting transfers between devices, __call__(): self.came.append(lax.ppermute(x, 'dp', pairs or self.pairs))  62.7 us
    ppermute x22, waiting for transfers between devices, __call__(): self.came.append(lax.ppermute(x, 'dp', pairs or self.pairs))  36.6 us
    dot_general x29, matrix products, dot(): return jnp.dot(a, b, preferred_element_type=jnp.float32)  14.3 us
    ppermute x1, starting transfers between devices, on_line(): guest_acts = lax.ppermute(coded, 'dp', TO_MIDDLE)  3.92 us
  transfers between devices with their start and end apart: 26, of which 9 were waited for; matrix products, arithmetic and copies ran while one was open for 18% of the time, Pallas kernels for 0%

profile of v1, /device:TPU:0, one launch (start us, length us, event | category | flops | bytes accessed | tf_op | source)
XLA Modules:
  0.0 135.0 jit_solution(7678093153789673467)
XLA Ops:
  0.0 3.0 %collective-permute-start = (bf16[1024,256]{1,0:T(8,128)(2,1)}, bf16[1024,256]{1,0:T(8,128)(2,1)S(1)}, u32[]{:S(2)}, u32[]{:S(2)}) collective-permute-start(bf16[1024,256]{1,0:T(8,128)(2,1)} %bitcast.129), channel_id=1, source_target_pairs={{0,4},{4,0},{8,12},{12,8},{1,5},{5,1},{9,13},{13,9},{2,6},{6,2},{1... | collective-permute-start | bytes 1572872 | tf_op jit(solution)/shard_map/ppermute | solution.py:62
  3.0 0.7 collective-permute-start.4
  3.7 1.8 %slice_bitcast_fusion = bf16[768,256]{1,0:T(8,128)(2,1)} fusion(bf16[1,3584,256]{2,1,0:T(8,128)(2,1)} %param.8), kind=kLoop, calls=%fused_computation.101 | loop fusion | bytes 786432 | tf_op jit(solution)/shard_map/slice | solution.py:110
  5.5 4.4 %collective-permute-start.1 = (bf16[768,256]{1,0:T(8,128)(2,1)}, bf16[768,256]{1,0:T(8,128)(2,1)}, u32[]{:S(2)}, u32[]{:S(2)}) collective-permute-start(bf16[768,256]{1,0:T(8,128)(2,1)} %slice_bitcast_fusion), channel_id=1, source_target_pairs={{0,4},{4,0},{8,12},{12,8},{1,5},{5,1},{9,13},{13,9},{2,6},{6,2},{1... | collective-permute-start | bytes 1179656 | tf_op jit(solution)/shard_map/ppermute | solution.py:62
  9.9 6.1 %collective-permute-done = bf16[1024,256]{1,0:T(8,128)(2,1)S(1)} collective-permute-done((bf16[1024,256]{1,0:T(8,128)(2,1)}, bf16[1024,256]{1,0:T(8,128)(2,1)S(1)}, u32[]{:S(2)}, u32[]{:S(2)}) %collective-permute-start) | collective-permute-done | bytes 524320 | tf_op jit(solution)/shard_map/ppermute | solution.py:62
  16.0 0.7 collective-permute-start.2
  16.7 0.7 fusion.148
  17.4 1.1 slice.139
  18.5 0.7 collective-permute-start.6
  19.2 1.3 slice_select_fusion
  20.5 6.6 %collective-permute-start.5 = (bf16[1024,256]{1,0:T(8,128)(2,1)S(1)}, bf16[1024,256]{1,0:T(8,128)(2,1)S(1)}, u32[]{:S(2)}, u32[]{:S(2)}) collective-permute-start(bf16[1024,256]{1,0:T(8,128)(2,1)S(1)} %slice_select_fusion), channel_id=1, source_target_pairs={{0,4},{4,0},{8,12},{12,8},{1,5},{5,1},{9,13},{13,9},{2,6},{6,2},{1... | collective-permute-start | bytes 1572872 | tf_op jit(solution)/shard_map/ppermute | solution.py:62
  27.1 1.7 %fusion.14 = f32[512,256]{1,0:T(8,128)S(1)} fusion(bf16[1024,256]{1,0:T(8,128)(2,1)S(1)} %collective-permute-done, bf16[1,512,4096]{2,1,0:T(8,128)(2,1)} %param.5, s32[]{:T(128)S(6)} %select_n.217), kind=kOutput, calls=%fused_computation.28 | convolution fusion | flops 268435456 | bytes 2097156 | tf_op jit(solution)/shard_map/dot_general | solution.py:36
  28.8 0.7 collective-permute-start.8
  29.6 8.9 %collective-permute-start.3 = (bf16[1024,256]{1,0:T(8,128)(2,1)S(1)}, bf16[1024,256]{1,0:T(8,128)(2,1)S(1)}, u32[]{:S(2)}, u32[]{:S(2)}) collective-permute-start(bf16[1024,256]{1,0:T(8,128)(2,1)S(1)} %slice_select_fusion.1), channel_id=1, source_target_pairs={{0,4},{4,0},{8,12},{12,8},{1,5},{5,1},{9,13},{13,9},{2,6},{6,2},{1... | collective-permute-start | bytes 1572872 | tf_op jit(solution)/shard_map/ppermute | solution.py:62
  38.5 1.7 %convolution_add_fusion.5 = f32[512,256]{1,0:T(8,128)S(1)} fusion(f32[512,256]{1,0:T(8,128)S(1)} %fusion.14, bf16[512,4096]{1,0:T(8,128)(2,1)} %bitcast.128, s32[]{:T(128)S(6)} %select_n.216, bf16[1,1024,256]{2,1,0:T(8,128)(2,1)S(1)} %copy-done.3), kind=kOutput, calls=%fused_computation.7 | convolution fusion | flops 268566528 | bytes 2621444 | tf_op jit(solution)/shard_map/dot_general | solution.py:36
  40.2 0.9 constant_dynamic-slice_fusion
  41.0 1.0 constant_dynamic-slice_fusion.11
  42.2 1.8 %collective-permute-start.7 = (bf16[768,256]{1,0:T(8,128)(2,1)S(1)}, bf16[768,256]{1,0:T(8,128)(2,1)S(1)}, u32[]{:S(2)}, u32[]{:S(2)}) collective-permute-start(bf16[768,256]{1,0:T(8,128)(2,1)S(1)} %maximum_select_fusion.4), channel_id=1, source_target_pairs={{0,4},{4,0},{8,12},{12,8},{1,5},{5,1},{9,13},{13,9},{2,6},{6,2},{1... | collective-permute-start | bytes 1179656 | tf_op jit(solution)/shard_map/ppermute | solution.py:62
  44.0 0.7 collective-permute-start.10
  44.8 0.7 collective-permute-start.12
  45.5 5.8 %collective-permute-done.3 = bf16[1024,256]{1,0:T(8,128)(2,1)S(1)} collective-permute-done((bf16[1024,256]{1,0:T(8,128)(2,1)S(1)}, bf16[1024,256]{1,0:T(8,128)(2,1)S(1)}, u32[]{:S(2)}, u32[]{:S(2)}) %collective-permute-start.3) | collective-permute-done | bytes 524320 | tf_op jit(solution)/shard_map/ppermute | solution.py:62
  51.3 1.1 constant_dynamic-slice_fusion.10
  52.5 6.8 %collective-permute-start.9 = (bf16[1024,256]{1,0:T(8,128)(2,1)S(1)}, bf16[1024,256]{1,0:T(8,128)(2,1)S(1)}, u32[]{:S(2)}, u32[]{:S(2)}) collective-permute-start(bf16[1024,256]{1,0:T(8,128)(2,1)S(1)} %maximum_select_fusion), channel_id=1, source_target_pairs={{0,4},{4,0},{8,12},{12,8},{1,5},{5,1},{9,13},{13,9},{2,6},{6,2},{1... | collective-permute-start | bytes 1572872 | tf_op jit(solution)/shard_map/ppermute | solution.py:62
  59.3 1.1 fusion
  60.7 1.5 %convolution_add_fusion.1 = f32[512,256]{1,0:T(8,128)S(1)} fusion(f32[512,256]{1,0:T(8,128)S(1)} %fusion, bf16[768,256]{1,0:T(8,128)(2,1)} %collective-permute-done.1, bf16[1,512,14336]{2,1,0:T(8,128)(2,1)S(1)} %copy-done.1, s32[]{:T(128)S(6)} %select_n.189), kind=kOutput, calls=%fused_computation.3 | convolution fusion | flops 201457664 | bytes 2228228 | tf_op jit(solution)/shard_map/dot_general | solution.py:36
  62.3 0.4 fusion.20
  62.7 0.2 convolution_add_fusion.13
  63.1 2.8 %collective-permute-start.11 = (bf16[1024,256]{1,0:T(8,128)(2,1)S(1)}, bf16[1024,256]{1,0:T(8,128)(2,1)S(1)}, u32[]{:S(2)}, u32[]{:S(2)}) collective-permute-start(bf16[1024,256]{1,0:T(8,128)(2,1)S(1)} %maximum_select_fusion.1), channel_id=1, source_target_pairs={{0,4},{4,0},{8,12},{12,8},{1,5},{5,1},{9,13},{13,9},{2,6},{6,2},{1... | collective-permute-start | bytes 1572872 | tf_op jit(solution)/shard_map/ppermute | solution.py:62
  65.9 0.5 convolution_add_fusion.4
  66.4 0.5 convolution_add_fusion.3
  66.8 1.6 %collective-permute-start.14 = (f32[512,256]{1,0:T(8,128)S(1)}, f32[512,256]{1,0:T(8,128)S(1)}, u32[]{:S(2)}, u32[]{:S(2)}) collective-permute-start(f32[512,256]{1,0:T(8,128)S(1)} %convolution_add_fusion.3), channel_id=1, source_target_pairs={{0,2},{2,0},{1,3},{3,1},{4,6},{6,4},{5,7},{7,5},{8,10},{10,8},{9,1... | collective-permute-start | bytes 1572872 | tf_op jit(solution)/shard_map/ppermute | solution.py:137
  68.4 0.7 collective-permute-start.15
  69.1 0.5 convolution_add_fusion.7
  69.5 0.4 fusion.39
  69.9 0.7 collective-permute-start.17
  70.6 0.7 collective-permute-start.19
  71.3 0.8 collective-permute-done.9
  72.2 14.0 %collective-permute-start.13 = (bf16[768,256]{1,0:T(8,128)(2,1)S(1)}, bf16[768,256]{1,0:T(8,128)(2,1)S(1)}, u32[]{:S(2)}, u32[]{:S(2)}) collective-permute-start(bf16[768,256]{1,0:T(8,128)(2,1)S(1)} %slice_select_fusion.2), channel_id=1, source_target_pairs={{0,4},{4,0},{8,12},{12,8},{1,5},{5,1},{9,13},{13,9},{2,6},{6,2},{1... | collective-permute-start | bytes 1179656 | tf_op jit(solution)/shard_map/ppermute | solution.py:62
  86.8 3.9 %collective-permute-start.23 = (s16[512,256]{1,0:T(8,128)(2,1)S(1)}, s16[512,256]{1,0:T(8,128)(2,1)S(1)}, u32[]{:S(2)}, u32[]{:S(2)}) collective-permute-start(s16[512,256]{1,0:T(8,128)(2,1)S(1)} %fusion.49), channel_id=1, source_target_pairs={{0,4},{12,8},{1,5},{13,9},{2,6},{14,10},{3,7},{15,11},{16,20},{28,... | collective-permute-start | bytes 786440 | tf_op jit(solution)/shard_map/ppermute | solution.py:142
  91.2 0.5 add_add_fusion
  91.9 0.2 fusion.6
  92.1 4.1 %collective-permute-done.13 = bf16[768,256]{1,0:T(8,128)(2,1)S(1)} collective-permute-done((bf16[768,256]{1,0:T(8,128)(2,1)S(1)}, bf16[768,256]{1,0:T(8,128)(2,1)S(1)}, u32[]{:S(2)}, u32[]{:S(2)}) %collective-permute-start.13) | collective-permute-done | bytes 393248 | tf_op jit(solution)/shard_map/ppermute | solution.py:62
  96.2 0.4 fusion.37
  96.6 0.4 fusion.35
  97.0 0.5 fusion.8
  97.7 2.1 %collective-permute-start.18 = (bf16[1024,256]{1,0:T(8,128)(2,1)S(1)}, bf16[1024,256]{1,0:T(8,128)(2,1)S(1)}, u32[]{:S(2)}, u32[]{:S(2)}) collective-permute-start(bf16[1024,256]{1,0:T(8,128)(2,1)S(1)} %maximum_select_fusion.2), channel_id=1, source_target_pairs={{0,4},{4,0},{8,12},{12,8},{1,5},{5,1},{9,13},{13,9},{2,6},{6,2},{1... | collective-permute-start | bytes 1572872 | tf_op jit(solution)/shard_map/ppermute | solution.py:62
  99.8 4.4 %collective-permute-done.16 = bf16[768,256]{1,0:T(8,128)(2,1)S(1)} collective-permute-done((bf16[768,256]{1,0:T(8,128)(2,1)S(1)}, bf16[768,256]{1,0:T(8,128)(2,1)S(1)}, u32[]{:S(2)}, u32[]{:S(2)}) %collective-permute-start.16) | collective-permute-done | bytes 393248 | tf_op jit(solution)/shard_map/ppermute | solution.py:62
  104.4 0.2 fusion.5
  104.6 0.4 convolution_add_fusion
  105.0 0.7 collective-permute-start.21
  105.9 4.2 %collective-permute-start.20 = (bf16[1024,256]{1,0:T(8,128)(2,1)S(1)}, bf16[1024,256]{1,0:T(8,128)(2,1)S(1)}, u32[]{:S(2)}, u32[]{:S(2)}) collective-permute-start(bf16[1024,256]{1,0:T(8,128)(2,1)S(1)} %maximum_select_fusion.3), channel_id=1, source_target_pairs={{0,4},{4,0},{8,12},{12,8},{1,5},{5,1},{9,13},{13,9},{2,6},{6,2},{1... | collective-permute-start | bytes 1572872 | tf_op jit(solution)/shard_map/ppermute | solution.py:62
  110.2 8.8 %collective-permute-done.18 = bf16[1024,256]{1,0:T(8,128)(2,1)S(1)} collective-permute-done((bf16[1024,256]{1,0:T(8,128)(2,1)S(1)}, bf16[1024,256]{1,0:T(8,128)(2,1)S(1)}, u32[]{:S(2)}, u32[]{:S(2)}) %collective-permute-start.18) | collective-permute-done | bytes 524320 | tf_op jit(solution)/shard_map/ppermute | solution.py:62
  119.0 0.5 fusion.10
  119.7 0.2 convolution_add_fusion.9
  120.1 1.3 collective-permute-start.22
  121.4 3.2 %collective-permute-done.20 = bf16[1024,256]{1,0:T(8,128)(2,1)S(1)} collective-permute-done((bf16[1024,256]{1,0:T(8,128)(2,1)S(1)}, bf16[1024,256]{1,0:T(8,128)(2,1)S(1)}, u32[]{:S(2)}, u32[]{:S(2)}) %collective-permute-start.20) | collective-permute-done | bytes 524320 | tf_op jit(solution)/shard_map/ppermute | solution.py:62
  124.8 0.3 bitcast_reduce_fusion
  125.1 1.3 collective-permute-start.24
  126.4 3.3 %collective-permute-done.22 = bf16[768,256]{1,0:T(8,128)(2,1)S(1)} collective-permute-done((bf16[768,256]{1,0:T(8,128)(2,1)S(1)}, bf16[768,256]{1,0:T(8,128)(2,1)S(1)}, u32[]{:S(2)}, u32[]{:S(2)}) %collective-permute-start.22) | collective-permute-done | bytes 393248 | tf_op jit(solution)/shard_map/ppermute | solution.py:62
  129.7 0.4 fusion.32
  130.1 0.5 fusion.3
  130.9 1.5 %collective-permute-start.25 = (f32[2,32]{1,0:T(2,128)S(1)}, f32[2,32]{1,0:T(2,128)S(1)}, u32[]{:S(2)}, u32[]{:S(2)}) collective-permute-start(f32[2,32]{1,0:T(2,128)S(1)} %reduce_sum.29), channel_id=1, source_target_pairs={{0,2},{2,0},{1,3},{3,1},{4,6},{6,4},{5,7},{7,5},{8,10},{10,8},{9,1... | collective-permute-start | bytes 776 | tf_op jit(solution)/shard_map/ppermute | solution.py:198
  132.4 2.1 %collective-permute-done.25 = f32[2,32]{1,0:T(2,128)S(1)} collective-permute-done((f32[2,32]{1,0:T(2,128)S(1)}, f32[2,32]{1,0:T(2,128)S(1)}, u32[]{:S(2)}, u32[]{:S(2)}) %collective-permute-start.25) | collective-permute-done | bytes 288 | tf_op jit(solution)/shard_map/ppermute | solution.py:198
  134.5 0.6 multiply_bitcast_fusion
  (62 shorter events, 3.7 us)
Async XLA Ops:
  0.0 28.7 %copy-start = (bf16[1,3584,256]{2,1,0:T(8,128)(2,1)S(1)}, bf16[1,3584,256]{2,1,0:T(8,128)(2,1)}, u32[]{:S(2)}) copy-start(bf16[1,3584,256]{2,1,0:T(8,128)(2,1)} %param.8) | copy-start | bytes 5505028
  0.0 16.0 %collective-permute-start = (bf16[1024,256]{1,0:T(8,128)(2,1)}, bf16[1024,256]{1,0:T(8,128)(2,1)S(1)}, u32[]{:S(2)}, u32[]{:S(2)}) collective-permute-start(bf16[1024,256]{1,0:T(8,128)(2,1)} %bitcast.129), channel_id=1, source_target_pairs={{0,4},{4,0},{8,12},{12,8},{1,5},{5,1},{9,13},{13,9},{2,6},{6,2},{1... | collective-permute-start | bytes 1572872 | tf_op jit(solution)/shard_map/ppermute | solution.py:62
  3.0 14.4 %collective-permute-start.4 = (bf16[1024,256]{1,0:T(8,128)(2,1)}, bf16[1024,256]{1,0:T(8,128)(2,1)S(1)}, u32[]{:S(2)}, u32[]{:S(2)}) collective-permute-start(bf16[1024,256]{1,0:T(8,128)(2,1)} %bitcast.130), channel_id=1, source_target_pairs={{4,8},{8,4},{5,9},{9,5},{6,10},{10,6},{7,11},{11,7},{20,24},{24,20... | collective-permute-start | bytes 1572872 | tf_op jit(solution)/shard_map/ppermute | solution.py:62
  5.5 21.6 %collective-permute-start.1 = (bf16[768,256]{1,0:T(8,128)(2,1)}, bf16[768,256]{1,0:T(8,128)(2,1)}, u32[]{:S(2)}, u32[]{:S(2)}) collective-permute-start(bf16[768,256]{1,0:T(8,128)(2,1)} %slice_bitcast_fusion), channel_id=1, source_target_pairs={{0,4},{4,0},{8,12},{12,8},{1,5},{5,1},{9,13},{13,9},{2,6},{6,2},{1... | collective-permute-start | bytes 1179656 | tf_op jit(solution)/shard_map/ppermute | solution.py:62
  16.0 12.7 %collective-permute-start.2 = (bf16[1024,256]{1,0:T(8,128)(2,1)S(1)}, bf16[1024,256]{1,0:T(8,128)(2,1)S(1)}, u32[]{:S(2)}, u32[]{:S(2)}) collective-permute-start(bf16[1024,256]{1,0:T(8,128)(2,1)S(1)} %collective-permute-done), channel_id=1, source_target_pairs={{4,8},{8,4},{5,9},{9,5},{6,10},{10,6},{7,11},{11,7},{20,24},{24,20... | collective-permute-start | bytes 1572872 | tf_op jit(solution)/shard_map/ppermute | solution.py:62
  17.4 21.0 %copy-start.3 = (bf16[1,1024,256]{2,1,0:T(8,128)(2,1)S(1)}, bf16[1,1024,256]{2,1,0:T(8,128)(2,1)}, u32[]{:S(2)}) copy-start(bf16[1,1024,256]{2,1,0:T(8,128)(2,1)} %param.7) | copy-start | bytes 1572868
  18.5 23.5 %collective-permute-start.6 = (bf16[768,256]{1,0:T(8,128)(2,1)S(1)}, bf16[768,256]{1,0:T(8,128)(2,1)S(1)}, u32[]{:S(2)}, u32[]{:S(2)}) collective-permute-start(bf16[768,256]{1,0:T(8,128)(2,1)S(1)} %slice.139), channel_id=1, source_target_pairs={{4,8},{8,4},{5,9},{9,5},{6,10},{10,6},{7,11},{11,7},{20,24},{24,20... | collective-permute-start | bytes 1179656 | tf_op jit(solution)/shard_map/ppermute | solution.py:62
  19.2 40.1 %copy-start.1 = (bf16[1,512,14336]{2,1,0:T(8,128)(2,1)S(1)}, bf16[1,512,14336]{2,1,0:T(8,128)(2,1)}, u32[]{:S(2)}) copy-start(bf16[1,512,14336]{2,1,0:T(8,128)(2,1)} %param.6) | copy-start | bytes 44040196
  20.5 19.7 %collective-permute-start.5 = (bf16[1024,256]{1,0:T(8,128)(2,1)S(1)}, bf16[1024,256]{1,0:T(8,128)(2,1)S(1)}, u32[]{:S(2)}, u32[]{:S(2)}) collective-permute-start(bf16[1024,256]{1,0:T(8,128)(2,1)S(1)} %slice_select_fusion), channel_id=1, source_target_pairs={{0,4},{4,0},{8,12},{12,8},{1,5},{5,1},{9,13},{13,9},{2,6},{6,2},{1... | collective-permute-start | bytes 1572872 | tf_op jit(solution)/shard_map/ppermute | solution.py:62
  28.8 15.9 %collective-permute-start.8 = (bf16[1024,256]{1,0:T(8,128)(2,1)S(1)}, bf16[1024,256]{1,0:T(8,128)(2,1)S(1)}, u32[]{:S(2)}, u32[]{:S(2)}) collective-permute-start(bf16[1024,256]{1,0:T(8,128)(2,1)S(1)} %slice.140), channel_id=1, source_target_pairs={{4,8},{8,4},{5,9},{9,5},{6,10},{10,6},{7,11},{11,7},{20,24},{24,20... | collective-permute-start | bytes 1572872 | tf_op jit(solution)/shard_map/ppermute | solution.py:62
  29.6 21.7 %collective-permute-start.3 = (bf16[1024,256]{1,0:T(8,128)(2,1)S(1)}, bf16[1024,256]{1,0:T(8,128)(2,1)S(1)}, u32[]{:S(2)}, u32[]{:S(2)}) collective-permute-start(bf16[1024,256]{1,0:T(8,128)(2,1)S(1)} %slice_select_fusion.1), channel_id=1, source_target_pairs={{0,4},{4,0},{8,12},{12,8},{1,5},{5,1},{9,13},{13,9},{2,6},{6,2},{1... | collective-permute-start | bytes 1572872 | tf_op jit(solution)/shard_map/ppermute | solution.py:62
  42.2 18.3 %collective-permute-start.7 = (bf16[768,256]{1,0:T(8,128)(2,1)S(1)}, bf16[768,256]{1,0:T(8,128)(2,1)S(1)}, u32[]{:S(2)}, u32[]{:S(2)}) collective-permute-start(bf16[768,256]{1,0:T(8,128)(2,1)S(1)} %maximum_select_fusion.4), channel_id=1, source_target_pairs={{0,4},{4,0},{8,12},{12,8},{1,5},{5,1},{9,13},{13,9},{2,6},{6,2},{1... | collective-permute-start | bytes 1179656 | tf_op jit(solution)/shard_map/ppermute | solution.py:62
  44.0 19.0 %collective-permute-start.10 = (bf16[1024,256]{1,0:T(8,128)(2,1)S(1)}, bf16[1024,256]{1,0:T(8,128)(2,1)S(1)}, u32[]{:S(2)}, u32[]{:S(2)}) collective-permute-start(bf16[1024,256]{1,0:T(8,128)(2,1)S(1)} %slice.152), channel_id=1, source_target_pairs={{4,8},{8,4},{5,9},{9,5},{6,10},{10,6},{7,11},{11,7},{20,24},{24,20... | collective-permute-start | bytes 1572872 | tf_op jit(solution)/shard_map/ppermute | solution.py:62
  44.8 25.2 %collective-permute-start.12 = (bf16[768,256]{1,0:T(8,128)(2,1)S(1)}, bf16[768,256]{1,0:T(8,128)(2,1)S(1)}, u32[]{:S(2)}, u32[]{:S(2)}) collective-permute-start(bf16[768,256]{1,0:T(8,128)(2,1)S(1)} %slice.154), channel_id=1, source_target_pairs={{4,8},{8,4},{5,9},{9,5},{6,10},{10,6},{7,11},{11,7},{20,24},{24,20... | collective-permute-start | bytes 1179656 | tf_op jit(solution)/shard_map/ppermute | solution.py:62
  52.5 19.6 %collective-permute-start.9 = (bf16[1024,256]{1,0:T(8,128)(2,1)S(1)}, bf16[1024,256]{1,0:T(8,128)(2,1)S(1)}, u32[]{:S(2)}, u32[]{:S(2)}) collective-permute-start(bf16[1024,256]{1,0:T(8,128)(2,1)S(1)} %maximum_select_fusion), channel_id=1, source_target_pairs={{0,4},{4,0},{8,12},{12,8},{1,5},{5,1},{9,13},{13,9},{2,6},{6,2},{1... | collective-permute-start | bytes 1572872 | tf_op jit(solution)/shard_map/ppermute | solution.py:62
  60.7 5.2 %copy-start.2 = (bf16[1,512,4096]{2,1,0:T(8,128)(2,1)S(1)}, bf16[1,512,4096]{2,1,0:T(8,128)(2,1)}, u32[]{:S(2)}) copy-start(bf16[1,512,4096]{2,1,0:T(8,128)(2,1)} %param.5) | copy-start | bytes 12582916
  63.1 23.2 %collective-permute-start.11 = (bf16[1024,256]{1,0:T(8,128)(2,1)S(1)}, bf16[1024,256]{1,0:T(8,128)(2,1)S(1)}, u32[]{:S(2)}, u32[]{:S(2)}) collective-permute-start(bf16[1024,256]{1,0:T(8,128)(2,1)S(1)} %maximum_select_fusion.1), channel_id=1, source_target_pairs={{0,4},{4,0},{8,12},{12,8},{1,5},{5,1},{9,13},{13,9},{2,6},{6,2},{1... | collective-permute-start | bytes 1572872 | tf_op jit(solution)/shard_map/ppermute | solution.py:62
  66.8 19.3 %collective-permute-start.14 = (f32[512,256]{1,0:T(8,128)S(1)}, f32[512,256]{1,0:T(8,128)S(1)}, u32[]{:S(2)}, u32[]{:S(2)}) collective-permute-start(f32[512,256]{1,0:T(8,128)S(1)} %convolution_add_fusion.3), channel_id=1, source_target_pairs={{0,2},{2,0},{1,3},{3,1},{4,6},{6,4},{5,7},{7,5},{8,10},{10,8},{9,1... | collective-permute-start | bytes 1572872 | tf_op jit(solution)/shard_map/ppermute | solution.py:137
  68.4 2.2 %collective-permute-start.15 = (bf16[768,256]{1,0:T(8,128)(2,1)}, bf16[768,256]{1,0:T(8,128)(2,1)S(1)}, u32[]{:S(2)}, u32[]{:S(2)}) collective-permute-start(bf16[768,256]{1,0:T(8,128)(2,1)} %collective-permute-done.1), channel_id=1, source_target_pairs={{4,8},{8,4},{5,9},{9,5},{6,10},{10,6},{7,11},{11,7},{20,24},{24,20... | collective-permute-start | bytes 1179656 | tf_op jit(solution)/shard_map/ppermute | solution.py:62
  69.9 27.6 %collective-permute-start.17 = (bf16[1024,256]{1,0:T(8,128)(2,1)S(1)}, bf16[1024,256]{1,0:T(8,128)(2,1)S(1)}, u32[]{:S(2)}, u32[]{:S(2)}) collective-permute-start(bf16[1024,256]{1,0:T(8,128)(2,1)S(1)} %collective-permute-done.5), channel_id=1, source_target_pairs={{4,8},{8,4},{5,9},{9,5},{6,10},{10,6},{7,11},{11,7},{20,24},{24,20... | collective-permute-start | bytes 1572872 | tf_op jit(solution)/shard_map/ppermute | solution.py:62
  70.6 34.4 %collective-permute-start.19 = (bf16[1024,256]{1,0:T(8,128)(2,1)S(1)}, bf16[1024,256]{1,0:T(8,128)(2,1)S(1)}, u32[]{:S(2)}, u32[]{:S(2)}) collective-permute-start(bf16[1024,256]{1,0:T(8,128)(2,1)S(1)} %collective-permute-done.3), channel_id=1, source_target_pairs={{4,8},{8,4},{5,9},{9,5},{6,10},{10,6},{7,11},{11,7},{20,24},{24,20... | collective-permute-start | bytes 1572872 | tf_op jit(solution)/shard_map/ppermute | solution.py:62
  72.2 24.0 %collective-permute-start.13 = (bf16[768,256]{1,0:T(8,128)(2,1)S(1)}, bf16[768,256]{1,0:T(8,128)(2,1)S(1)}, u32[]{:S(2)}, u32[]{:S(2)}) collective-permute-start(bf16[768,256]{1,0:T(8,128)(2,1)S(1)} %slice_select_fusion.2), channel_id=1, source_target_pairs={{0,4},{4,0},{8,12},{12,8},{1,5},{5,1},{9,13},{13,9},{2,6},{6,2},{1... | collective-permute-start | bytes 1179656 | tf_op jit(solution)/shard_map/ppermute | solution.py:62
  86.6 17.6 %collective-permute-start.16 = (bf16[768,256]{1,0:T(8,128)(2,1)S(1)}, bf16[768,256]{1,0:T(8,128)(2,1)S(1)}, u32[]{:S(2)}, u32[]{:S(2)}) collective-permute-start(bf16[768,256]{1,0:T(8,128)(2,1)S(1)} %maximum_select_fusion.5), channel_id=1, source_target_pairs={{0,4},{4,0},{8,12},{12,8},{1,5},{5,1},{9,13},{13,9},{2,6},{6,2},{1... | collective-permute-start | bytes 1179656 | tf_op jit(solution)/shard_map/ppermute | solution.py:62
  86.8 38.0 %collective-permute-start.23 = (s16[512,256]{1,0:T(8,128)(2,1)S(1)}, s16[512,256]{1,0:T(8,128)(2,1)S(1)}, u32[]{:S(2)}, u32[]{:S(2)}) collective-permute-start(s16[512,256]{1,0:T(8,128)(2,1)S(1)} %fusion.49), channel_id=1, source_target_pairs={{0,4},{12,8},{1,5},{13,9},{2,6},{14,10},{3,7},{15,11},{16,20},{28,... | collective-permute-start | bytes 786440 | tf_op jit(solution)/shard_map/ppermute | solution.py:142
  97.7 21.3 %collective-permute-start.18 = (bf16[1024,256]{1,0:T(8,128)(2,1)S(1)}, bf16[1024,256]{1,0:T(8,128)(2,1)S(1)}, u32[]{:S(2)}, u32[]{:S(2)}) collective-permute-start(bf16[1024,256]{1,0:T(8,128)(2,1)S(1)} %maximum_select_fusion.2), channel_id=1, source_target_pairs={{0,4},{4,0},{8,12},{12,8},{1,5},{5,1},{9,13},{13,9},{2,6},{6,2},{1... | collective-permute-start | bytes 1572872 | tf_op jit(solution)/shard_map/ppermute | solution.py:62
  105.0 15.0 %collective-permute-start.21 = (bf16[768,256]{1,0:T(8,128)(2,1)S(1)}, bf16[768,256]{1,0:T(8,128)(2,1)S(1)}, u32[]{:S(2)}, u32[]{:S(2)}) collective-permute-start(bf16[768,256]{1,0:T(8,128)(2,1)S(1)} %collective-permute-done.13), channel_id=1, source_target_pairs={{4,8},{8,4},{5,9},{9,5},{6,10},{10,6},{7,11},{11,7},{20,24},{24,20... | collective-permute-start | bytes 1179656 | tf_op jit(solution)/shard_map/ppermute | solution.py:62
  105.9 18.7 %collective-permute-start.20 = (bf16[1024,256]{1,0:T(8,128)(2,1)S(1)}, bf16[1024,256]{1,0:T(8,128)(2,1)S(1)}, u32[]{:S(2)}, u32[]{:S(2)}) collective-permute-start(bf16[1024,256]{1,0:T(8,128)(2,1)S(1)} %maximum_select_fusion.3), channel_id=1, source_target_pairs={{0,4},{4,0},{8,12},{12,8},{1,5},{5,1},{9,13},{13,9},{2,6},{6,2},{1... | collective-permute-start | bytes 1572872 | tf_op jit(solution)/shard_map/ppermute | solution.py:62
  120.1 9.7 %collective-permute-start.22 = (bf16[768,256]{1,0:T(8,128)(2,1)S(1)}, bf16[768,256]{1,0:T(8,128)(2,1)S(1)}, u32[]{:S(2)}, u32[]{:S(2)}) collective-permute-start(bf16[768,256]{1,0:T(8,128)(2,1)S(1)} %collective-permute-done.21), channel_id=1, source_target_pairs={{4,0},{8,12},{5,1},{9,13},{6,2},{10,14},{7,3},{11,15},{20,16},{24,... | collective-permute-start | bytes 1179656 | tf_op jit(solution)/shard_map/ppermute | solution.py:62
  125.1 5.6 %collective-permute-start.24 = (f32[2,256]{1,0:T(2,128)S(1)}, f32[2,256]{1,0:T(2,128)S(1)}, u32[]{:S(2)}, u32[]{:S(2)}) collective-permute-start(f32[2,256]{1,0:T(2,128)S(1)} %bitcast_reduce_fusion), channel_id=1, source_target_pairs={{4,0},{8,12},{5,1},{9,13},{6,2},{10,14},{7,3},{11,15},{20,16},{24,... | collective-permute-start | bytes 6152 | tf_op jit(solution)/shard_map/ppermute | solution.py:193
  130.9 3.6 %collective-permute-start.25 = (f32[2,32]{1,0:T(2,128)S(1)}, f32[2,32]{1,0:T(2,128)S(1)}, u32[]{:S(2)}, u32[]{:S(2)}) collective-permute-start(f32[2,32]{1,0:T(2,128)S(1)} %reduce_sum.29), channel_id=1, source_target_pairs={{0,2},{2,0},{1,3},{3,1},{4,6},{6,4},{5,7},{7,5},{8,10},{10,8},{9,1... | collective-permute-start | bytes 776 | tf_op jit(solution)/shard_map/ppermute | solution.py:198
